TPU v7x, 512 devices: a whole 4x4x16 slice. The times are simulated.
512 devices in a mesh: group: 32 (over y_lo, z), tensor: 16 (over y_hi, x, core).
Axes of the slice: x: 4, y: 4 (y_hi: 2, y_lo: 2; y = y_hi * 2 + y_lo), z: 16, core: 2. Of those that a mesh axis runs over, the one named last changes fastest.
Arguments:
- queries: bfloat16 [4, 256, 4096], P(None, 'group', 'tensor')
- key_cache_rows: bfloat16 [256, 16, 512, 128], P('group', 'tensor'), as said below
- value_cache_rows: bfloat16 [256, 16, 512, 128], P('group', 'tensor'), as said below
- step_keys: bfloat16 [4, 256, 16, 128], P(None, 'group', 'tensor'), as said below
- step_values: bfloat16 [4, 256, 16, 128], P(None, 'group', 'tensor'), as said below
- lengths: int32 [256], P('group'), may hold values from 2 to 512, as said below
- output_weight: bfloat16 [4096, 5120], P('tensor'), may hold values from -0.125 to 0.125
- adapter_down_weight: bfloat16 [4096, 64], P('tensor', 'group'), may hold values from -0.09375 to 0.09375
- adapter_up_weight: bfloat16 [64, 5120], P('group', 'tensor'), may hold values from -0.75 to 0.75
Outputs:
- projected: bfloat16 [4, 256, 5120], P(None, 'group', 'tensor')
Inputs may be any that keep to these rules, and one draw needn't show every extreme that they name: `lengths`: each sequence has from 2 to 512 cached positions; some sequence has exactly 512 and some exactly 2. `key_cache_rows`: copies g and g' are equal when g // 4 == g' // 4. `value_cache_rows`: copies g and g' are equal when g // 4 == g' // 4. `step_keys`: copies g and g' are equal when g // 4 == g' // 4. `step_values`: copies g and g' are equal when g // 4 == g' // 4.
All inputs are finite; a program needn't handle non-finite values.
Results may differ from a plain program's by a relative error of at most 0.0057.
Values may be sent and summed in bfloat16 or wider, within the bound.
A program may use at most 64 MiB of HBM per device.

v0:
```python
import jax
import jax.numpy as jnp
from jax import lax
from jax.sharding import PartitionSpec as P

HEAD_SIZE = 128
QH = 2


def attend_local(queries, key_cache_rows, value_cache_rows, step_keys, step_values, lengths):
    step_count, row_count = (queries.shape[0], queries.shape[1])
    cache_len = key_cache_rows.shape[2]
    score_scale = HEAD_SIZE ** (-0.5)
    query_heads = queries.reshape(step_count, row_count, QH, HEAD_SIZE)
    cached = (
        jnp.einsum(
            "srqd,rld->srql", query_heads, key_cache_rows[:, 0], preferred_element_type=jnp.float32
        )
        * score_scale
    )
    in_cache = (
        lax.broadcasted_iota(jnp.int32, (1, row_count, 1, cache_len), 3)
        < lengths[None, :, None, None]
    )
    cached = jnp.where(in_cache, cached, jnp.float32(-1e30))
    recent = (
        jnp.einsum(
            "srqd,trd->srqt", query_heads, step_keys[:, :, 0], preferred_element_type=jnp.float32
        )
        * score_scale
    )
    causal = lax.broadcasted_iota(jnp.int32, (step_count, step_count), 1) <= lax.broadcasted_iota(
        jnp.int32, (step_count, step_count), 0
    )
    recent = jnp.where(causal[:, None, None, :], recent, jnp.float32(-1e30))
    row_top = jnp.maximum(
        jnp.max(cached, axis=-1, keepdims=True), jnp.max(recent, axis=-1, keepdims=True)
    )
    cached_exp = jnp.exp(cached - row_top)
    recent_exp = jnp.exp(recent - row_top)
    weight_sum = jnp.sum(cached_exp, axis=-1, keepdims=True) + jnp.sum(
        recent_exp, axis=-1, keepdims=True
    )
    cached_w = (cached_exp / weight_sum).astype(jnp.bfloat16)
    recent_w = (recent_exp / weight_sum).astype(jnp.bfloat16)
    mixed = jnp.einsum(
        "srql,rld->srqd", cached_w, value_cache_rows[:, 0], preferred_element_type=jnp.float32
    )
    mixed = mixed + jnp.einsum(
        "srqt,trd->srqd", recent_w, step_values[:, :, 0], preferred_element_type=jnp.float32
    )
    return mixed.astype(jnp.bfloat16).reshape(step_count * row_count, QH * HEAD_SIZE)


def on_device(
    queries,
    key_cache_rows,
    value_cache_rows,
    step_keys,
    step_values,
    lengths,
    output_weight,
    adapter_down_weight,
    adapter_up_weight,
):
    step_count, row_count = (queries.shape[0], queries.shape[1])
    width = output_weight.shape[1]
    attention_output = attend_local(
        queries, key_cache_rows, value_cache_rows, step_keys, step_values, lengths
    )
    down_columns = lax.all_gather(adapter_down_weight, "group", axis=1, tiled=True)
    up_weight_rows = lax.all_gather(adapter_up_weight, "group", axis=0, tiled=True)
    low_rank_output = jnp.dot(attention_output, down_columns, preferred_element_type=jnp.float32)
    partial_value = jnp.dot(attention_output, output_weight, preferred_element_type=jnp.float32)
    up_whole = lax.all_gather(up_weight_rows, "tensor", axis=1, tiled=True)
    partial_value = partial_value + 2.0 * jnp.dot(
        low_rank_output, up_whole.astype(jnp.float32), precision=lax.Precision.HIGHEST
    )
    partial_value = partial_value.reshape(step_count, row_count, width)
    shares = jnp.stack(
        [
            lax.psum_scatter(partial_value[index], "tensor", scatter_dimension=1, tiled=True)
            for index in range(step_count)
        ]
    )
    return shares.astype(jnp.bfloat16)


def solution(mesh):
    return jax.shard_map(
        on_device,
        mesh=mesh,
        in_specs=(
            P(None, "group", "tensor"),
            P("group", "tensor", None, None),
            P("group", "tensor", None, None),
            P(None, "group", "tensor", None),
            P(None, "group", "tensor", None),
            P("group"),
            P("tensor", None),
            P("tensor", "group"),
            P("group", "tensor"),
        ),
        out_specs=P(None, "group", "tensor"),
        check_vma=False,
    )
```

profile of v0, /device:TPU:1, one launch (start us, length us, event | category | flops | bytes accessed | tf_op | source)
XLA Modules:
  0.0 568.1 jit_solution(15525834201552716265)
XLA Ops:
  6.5 0.9 iota_compare_fusion
  7.4 56.1 %all-gather = bf16[32,2,256]{2,1,0:T(2,128)(2,1)S(1)} all-gather(bf16[1,2,256]{2,1,0:T(2,128)(2,1)} %bitcast.81), channel_id=1, replica_groups=mesh['group'=32,'tensor'=16] {'group'}, dimensions={0}, use_global_device_ids=true | all-gather | bytes 33792 | tf_op jit(solution)/shard_map/all_gather | solution.py:71
  63.5 45.3 %all-gather.1 = bf16[32,2,320]{2,1,0:T(2,128)(2,1)S(1)} all-gather(bf16[1,2,320]{2,1,0:T(2,128)(2,1)} %bitcast.80), channel_id=1, replica_groups=mesh['group'=32,'tensor'=16] {'group'}, dimensions={0}, use_global_device_ids=true | all-gather | bytes 42240 | tf_op jit(solution)/shard_map/all_gather | solution.py:72
  108.9 1.0 fusion.28
  110.0 1.7 fusion.27
  111.7 0.2 fusion.10
  111.9 1.5 fusion.7
  113.5 0.2 fusion.6
  113.7 0.1 fusion.14
  113.8 1.4 fusion.16
  115.2 54.1 %all-gather.2 = bf16[16,320,64]{1,2,0:T(8,128)(2,1)S(1)} all-gather(bf16[1,320,64]{1,2,0:T(8,128)(2,1)S(1)} %bitcast.71), channel_id=1, replica_groups=mesh['group'=32,'tensor'=16] {'tensor'}, dimensions={0}, use_global_device_ids=true | all-gather | bytes 696320 | tf_op jit(solution)/shard_map/all_gather | solution.py:75
  169.4 0.5 copy.34
  169.8 1.5 reshape.59
  171.3 1.7 fusion
  173.1 2.3 copy.44
  175.4 0.0 reduce-scatter.13.cloned.1.call-update
  175.4 0.0 reduce-scatter.19.cloned.1.call-start
  175.5 2.2 copy.50
  177.7 0.0 reduce-scatter.19.cloned.1.call-update
  177.8 0.0 reduce-scatter.17.cloned.1.call-start
  177.8 2.3 copy.48
  180.1 0.0 reduce-scatter.15.cloned.1.call-start
  180.2 2.3 copy.46
  182.4 75.4 %reduce-scatter.13.cloned.1.call-done = f32[320,8]{1,0:T(8,128)} async-done(((f32[5120,8]{1,0:T(8,128)}), f32[320,8]{1,0:T(8,128)}) %reduce-scatter.13.cloned.1.call-update) | async-done | bytes 10256
  257.8 1.0 copy.45
  258.8 100.1 %reduce-scatter.19.cloned.1.call-done = f32[320,8]{1,0:T(8,128)} async-done(((f32[5120,8]{1,0:T(8,128)}), f32[320,8]{1,0:T(8,128)}) %reduce-scatter.19.cloned.1.call-update) | async-done | bytes 10256
  358.9 1.0 copy.51
  359.9 99.2 %reduce-scatter.17.cloned.1.call-done = f32[320,8]{1,0:T(8,128)} async-done(((f32[5120,8]{1,0:T(8,128)}), f32[320,8]{1,0:T(8,128)}) %reduce-scatter.17.cloned.1.call-update) | async-done | bytes 10256
  459.1 1.0 copy.49
  460.1 99.8 %reduce-scatter.15.cloned.1.call-done = f32[320,8]{1,0:T(8,128)} async-done(((f32[5120,8]{1,0:T(8,128)}), f32[320,8]{1,0:T(8,128)}) %reduce-scatter.15.cloned.1.call-update) | async-done | bytes 10256
  559.9 1.0 copy.47
  560.9 0.6 pad_maximum_fusion
  (14 shorter events, 0.2 us)
Async XLA Ops:
  6.5 107.3 %copy-start = (bf16[256,5120]{1,0:T(8,128)(2,1)S(1)}, bf16[256,5120]{1,0:T(8,128)(2,1)}, u32[]{:S(2)}) copy-start(bf16[256,5120]{1,0:T(8,128)(2,1)} %param.15) | copy-start | bytes 7864324
  6.5 106.9 %copy-start.1 = (bf16[4,8,1,128]{3,1,2,0:T(8,128)(2,1)S(1)}, bf16[4,8,1,128]{3,1,2,0:T(8,128)(2,1)}, u32[]{:S(2)}) copy-start(bf16[4,8,1,128]{3,1,2,0:T(8,128)(2,1)} %param.13) | copy-start | bytes 24580
  6.5 251.3 %reduce-scatter.13.cloned.1.call-start = ((), (), s32[]{:S(2)}) async-start(), calls=%async_computation.4 | async-start | bytes 2785280
  175.4 183.5 %reduce-scatter.19.cloned.1.call-start = ((), (), s32[]{:S(2)}) async-start(), calls=%async_computation.7 | async-start | bytes 2785280
  177.8 281.3 %reduce-scatter.17.cloned.1.call-start = ((), (), s32[]{:S(2)}) async-start(), calls=%async_computation.6 | async-start | bytes 2785280
  180.1 379.8 %reduce-scatter.15.cloned.1.call-start = ((), (), s32[]{:S(2)}) async-start(), calls=%async_computation.5 | async-start | bytes 2785280
Sparse Core Ops, SparseCore 0:
  175.6 82.1 reduce-scatter.12
  263.4 95.4 reduce-scatter.18
  363.8 95.3 reduce-scatter.16
  464.5 95.3 reduce-scatter.14
where the time goes:
time: 569 us; the launch traced here: 568 us
  waiting for transfers between devices  375 us (66%)
  blocking collectives  156 us (27%)
  local copies, waits for them, and re-layouts  15.1 us (3%)
  between operations  13.2 us (2%)
  matrix products  7.71 us (1%)
    unnamed x8, waiting for transfers between devices  375 us
    all_gather x1, blocking collectives, on_device(): lax.all_gather(adapter_down_weight, 'group', axis=1, tiled=True)  56.1 us
    all_gather x1, blocking collectives, on_device(): up_whole = lax.all_gather(up_weight_rows, 'tensor', axis=1, tiled=True)  54.1 us
    all_gather x1, blocking collectives, on_device(): lax.all_gather(adapter_up_weight, 'group', axis=0, tiled=True)  45.3 us
    unnamed x15, local copies, waits for them, and re-layouts  14.6 us
  transfers between devices with their start and end apart: 4, of which 4 were waited for; matrix products, arithmetic and copies ran while one was open for 2% of the time, Pallas kernels for 0%

commit v1 on v0

v1 whole, which is shorter than its diff:
```python
import functools
import math

import jax
import jax.numpy as jnp
from jax import lax
from jax.experimental import pallas as pl
from jax.experimental.pallas import tpu as pltpu
from jax.sharding import PartitionSpec as P

MESH = pl.DeviceIdType.MESH
HEAD_SIZE = 128
QH = 2
EXP2_SCALE = HEAD_SIZE**-0.5 / math.log(2.0)
NEG = -1e30
VMEM_BYTES = 63 * 1024 * 1024


def nt_dot(a, b):
    return lax.dot_general(a, b, (((1,), (1,)), ((), ())), preferred_element_type=jnp.float32)


def kernel(
    groups,
    tensors,
    q_hbm,
    k_hbm,
    v_hbm,
    sk_hbm,
    sv_hbm,
    len_hbm,
    w_hbm,
    down_hbm,
    up_hbm,
    out_ref,
    q_v,
    k_v,
    v_v,
    sk_v,
    sv_v,
    len_v,
    w_v,
    down_v,
    up_v,
    gath,
    factors,
    keep,
    send1,
    recv1,
    send2,
    recv2,
    small_sem,
    k_sem,
    v_sem,
    w_sem,
    gsend_sem,
    grecv_sem,
    s1_sem,
    r1_sem,
    s2_sem,
    r2_sem,
):
    steps, rows, _ = q_v.shape
    cache = k_v.shape[0]
    toks = steps * rows
    cols = out_ref.shape[2]
    depth = down_v.shape[1]
    chips = tensors // 2
    rank = factors.shape[0]

    g = lax.axis_index("group")
    t = lax.axis_index("tensor")
    chip = t // 2
    core = t % 2

    smalls = [
        pltpu.make_async_copy(src, dst, small_sem.at[i])
        for i, (src, dst) in enumerate(
            [
                (down_hbm, down_v),
                (up_hbm, up_v),
                (q_hbm, q_v),
                (sk_hbm, sk_v),
                (sv_hbm, sv_v),
                (len_hbm, len_v),
            ]
        )
    ]
    for c in smalls:
        c.start()
    k_copies = [
        pltpu.make_async_copy(k_hbm.at[r], k_v.at[:, pl.ds(r * HEAD_SIZE, HEAD_SIZE)], k_sem.at[r])
        for r in range(rows)
    ]
    v_copies = [
        pltpu.make_async_copy(v_hbm.at[r], v_v.at[pl.ds(r * cache, cache)], v_sem.at[r])
        for r in range(rows)
    ]
    pair = 2 * cols

    def chunk_at(k):
        return lax.rem(chip + k + 1, chips)

    w_copies = [
        pltpu.make_async_copy(
            w_hbm.at[:, pl.ds(pl.multiple_of(chunk_at(k) * pair, 128), pair)], w_v.at[k], w_sem.at[k]
        )
        for k in range(chips)
    ]
    for c in k_copies + v_copies + w_copies:
        c.start()

    barrier = pltpu.get_barrier_semaphore()

    def greet_group(d, carry):
        pl.semaphore_signal(
            barrier, inc=1, device_id={"group": lax.rem(g + d, groups)}, device_id_type=MESH
        )
        return carry

    lax.fori_loop(1, groups, greet_group, 0)
    pl.semaphore_signal(barrier, inc=1, device_id={"tensor": t + 1 - 2 * core}, device_id_type=MESH)
    for k in range(chips - 1):
        pl.semaphore_signal(
            barrier, inc=1, device_id={"tensor": chunk_at(k) * 2 + core}, device_id_type=MESH
        )
    own = groups - 1
    smalls[0].wait()
    smalls[1].wait()
    gath[own, :, 0:depth] = down_v[...]
    gath[own, :, depth : depth + cols] = up_v[...]
    gath[own, :, depth + cols :] = jnp.zeros(
        (gath.shape[1], gath.shape[2] - depth - cols), gath.dtype
    )
    pl.semaphore_wait(barrier, (groups - 1) + 1 + (chips - 1))

    def send_factors(d, carry):
        pltpu.make_async_remote_copy(
            src_ref=gath.at[own],
            dst_ref=gath.at[d],
            send_sem=gsend_sem,
            recv_sem=grecv_sem,
            device_id={"group": lax.rem(g + d + 1, groups)},
            device_id_type=MESH,
        ).start()
        return carry

    lax.fori_loop(0, groups - 1, send_factors, 0)

    for c in smalls[2:]:
        c.wait()
    q32 = jnp.concatenate([q_v[s].astype(jnp.float32) for s in range(steps)], axis=0)
    q64 = jnp.concatenate([q32[:, h * HEAD_SIZE : (h + 1) * HEAD_SIZE] for h in range(QH)], axis=0)
    height = QH * toks
    row_of = lax.broadcasted_iota(jnp.int32, (height, 1), 0) % rows
    step_of = (lax.broadcasted_iota(jnp.int32, (height, 1), 0) // rows) % steps
    q_wide = jnp.concatenate(
        [jnp.where(row_of == r, q64, 0.0).astype(jnp.bfloat16) for r in range(rows)], axis=1
    )
    sk = jnp.concatenate([sk_v[s].astype(jnp.float32) for s in range(steps)], axis=0)
    sv = jnp.concatenate([sv_v[s].astype(jnp.float32) for s in range(steps)], axis=0)
    recent = nt_dot(q64.astype(jnp.bfloat16), sk.astype(jnp.bfloat16))
    col = lax.broadcasted_iota(jnp.int32, (height, toks), 1)
    recent = jnp.where((col % rows == row_of) & (col // rows <= step_of), recent, NEG)
    lane = lax.broadcasted_iota(jnp.int32, (rows, rows), 1)
    sub = lax.broadcasted_iota(jnp.int32, (rows, rows), 0)
    lens = jnp.sum(
        jnp.where(lane == sub, jnp.broadcast_to(len_v[...], (rows, rows)), 0).astype(jnp.float32),
        axis=1,
        keepdims=True,
    )
    lens = jnp.concatenate([lens] * (QH * steps), axis=0)
    for c in k_copies:
        c.wait()
    cached = nt_dot(q_wide, k_v[...])
    position = lax.broadcasted_iota(jnp.int32, (height, cache), 1).astype(jnp.float32)
    cached = jnp.where(position < lens, cached, NEG)
    top = jnp.maximum(
        jnp.max(cached, axis=1, keepdims=True), jnp.max(recent, axis=1, keepdims=True)
    )
    cached = jnp.exp2((cached - top) * EXP2_SCALE)
    recent = jnp.exp2((recent - top) * EXP2_SCALE)
    norm = 1.0 / (
        jnp.sum(cached, axis=1, keepdims=True) + jnp.sum(recent, axis=1, keepdims=True)
    )
    cached = cached * norm
    recent = (recent * norm).astype(jnp.bfloat16)
    for c in v_copies:
        c.wait()
    mixed = jnp.dot(recent, sv.astype(jnp.bfloat16), preferred_element_type=jnp.float32)
    weights = jnp.concatenate(
        [jnp.where(row_of == r, cached, 0.0).astype(jnp.bfloat16) for r in range(rows)], axis=1
    )
    mixed = mixed + jnp.dot(weights, v_v[...], preferred_element_type=jnp.float32)
    attended = jnp.concatenate([mixed[h * toks : (h + 1) * toks] for h in range(QH)], axis=1)
    attended = attended.astype(jnp.bfloat16)

    others = gath.at[pl.ds(0, groups - 1)]
    pltpu.make_async_copy(others, others, grecv_sem).wait()
    per = gath.shape[1]
    for i in range(groups):
        factors[per * i : per * (i + 1), :] = gath[i].astype(jnp.float32)
    low = nt_dot(attended, factors[:, 0:depth].astype(jnp.bfloat16))

    to_partner = []
    for k in range(chips):
        w_copies[k].wait()
        part = jnp.dot(attended, w_v[k], preferred_element_type=jnp.float32)
        first, second = part[:, :cols], part[:, cols:]
        mine = jnp.where(core == 0, first, second)
        theirs = jnp.where(core == 0, second, first)
        keep[k, :, :] = jnp.concatenate([mine, low], axis=1)
        send1[k, :, :] = jnp.concatenate([theirs, low], axis=1).astype(jnp.bfloat16)
        copy = pltpu.make_async_remote_copy(
            src_ref=send1.at[k],
            dst_ref=recv1.at[k],
            send_sem=s1_sem.at[k],
            recv_sem=r1_sem.at[k],
            device_id={"tensor": t + 1 - 2 * core},
            device_id_type=MESH,
        )
        copy.start()
        to_partner.append(copy)

    to_chips = []
    for k in range(chips):
        to_partner[k].wait_recv()
        both = keep[k] + recv1[k].astype(jnp.float32)
        if k < chips - 1:
            send2[k, :, :] = both.astype(jnp.bfloat16)
            copy = pltpu.make_async_remote_copy(
                src_ref=send2.at[k],
                dst_ref=recv2.at[k],
                send_sem=s2_sem.at[k],
                recv_sem=r2_sem.at[k],
                device_id={"tensor": chunk_at(k) * 2 + core},
                device_id_type=MESH,
            )
            copy.start()
            to_chips.append(copy)
        else:
            total = both

    up = factors[:, depth : depth + cols].astype(jnp.bfloat16)
    for k in range(chips - 1):
        to_chips[k].wait_recv()
        total = total + recv2[k].astype(jnp.float32)
    low = total[:, cols : cols + rank]
    high = low.astype(jnp.bfloat16)
    rest = (low - high.astype(jnp.float32)).astype(jnp.bfloat16)
    delta = jnp.dot(high, up, preferred_element_type=jnp.float32) + jnp.dot(
        rest, up, preferred_element_type=jnp.float32
    )
    result = (total[:, :cols] + 2.0 * delta).astype(out_ref.dtype)
    for s in range(steps):
        out_ref[s, :, :] = result[s * rows : (s + 1) * rows]

    pltpu.make_async_copy(others, others, gsend_sem).wait()
    for copy in to_partner + to_chips:
        copy.wait_send()


def on_device(mesh_shape, queries, keys, values, step_keys, step_values, lengths, weight, down, up):
    groups, tensors = mesh_shape
    steps, rows, width = queries.shape
    cache = keys.shape[2]
    depth, per = down.shape
    cols = up.shape[1]
    chips = tensors // 2
    toks = steps * rows
    rank = per * groups
    chunk = cols + rank
    message = -(-(depth + cols) // 128) * 128
    bf16, f32 = jnp.bfloat16, jnp.float32
    hbm = pl.BlockSpec(memory_space=pltpu.HBM)
    dma = pltpu.SemaphoreType.DMA
    return pl.pallas_call(
        functools.partial(kernel, groups, tensors),
        out_shape=jax.ShapeDtypeStruct((steps, rows, cols), bf16),
        in_specs=[hbm] * 9,
        out_specs=pl.BlockSpec(memory_space=pltpu.VMEM),
        scratch_shapes=[
            pltpu.VMEM((steps, rows, width), bf16),
            pltpu.VMEM((cache, rows * HEAD_SIZE), bf16),
            pltpu.VMEM((rows * cache, HEAD_SIZE), bf16),
            pltpu.VMEM((steps, rows, HEAD_SIZE), bf16),
            pltpu.VMEM((steps, rows, HEAD_SIZE), bf16),
            pltpu.VMEM((1, rows), jnp.int32),
            pltpu.VMEM((chips, depth, 2 * cols), bf16),
            pltpu.VMEM((per, depth), bf16),
            pltpu.VMEM((per, cols), bf16),
            pltpu.VMEM((groups, per, message), bf16),
            pltpu.VMEM((rank, message), f32),
            pltpu.VMEM((chips, toks, chunk), f32),
            pltpu.VMEM((chips, toks, chunk), bf16),
            pltpu.VMEM((chips, toks, chunk), bf16),
            pltpu.VMEM((chips - 1, toks, chunk), bf16),
            pltpu.VMEM((chips - 1, toks, chunk), bf16),
            dma((6,)),
            dma((rows,)),
            dma((rows,)),
            dma((chips,)),
            dma,
            dma,
            dma((chips,)),
            dma((chips,)),
            dma((chips - 1,)),
            dma((chips - 1,)),
        ],
        compiler_params=pltpu.CompilerParams(
            collective_id=0, has_side_effects=True, vmem_limit_bytes=VMEM_BYTES
        ),
    )(
        queries,
        keys[:, 0],
        values[:, 0],
        step_keys[:, :, 0],
        step_values[:, :, 0],
        lengths[None, :],
        weight,
        down.T,
        up,
    )


def solution(mesh):
    return jax.shard_map(
        functools.partial(on_device, (mesh.shape["group"], mesh.shape["tensor"])),
        mesh=mesh,
        in_specs=(
            P(None, "group", "tensor"),
            P("group", "tensor", None, None),
            P("group", "tensor", None, None),
            P(None, "group", "tensor", None),
            P(None, "group", "tensor", None),
            P("group"),
            P("tensor", None),
            P("tensor", "group"),
            P("group", "tensor"),
        ),
        out_specs=P(None, "group", "tensor"),
        check_vma=False,
    )
```

time: 569 us -> 35.3 us (0.06)
  waiting for transfers between devices: 375 us -> 0 us
  blocking collectives: 156 us -> 0 us
  Pallas kernels: 0 us -> 33.7 us
  local copies, waits for them, and re-layouts: 15.1 us -> 1.35 us
  between operations: 13.2 us -> 0.01 us
  matrix products: 7.71 us -> 0 us
    unnamed x8 -> x0, waiting for transfers between devices: 375 us -> none
    all_gather x3 -> x0, blocking collectives: 156 us -> none  [the longest x1 56.1 us: on_device(): lax.all_gather(adapter_down_weight, 'group', axis=1, tiled=True)]
    pallas_call x0 -> x1, Pallas kernels: none -> 33.7 us  [on_device(): pl.pallas_call(functools.partial(kernel, groups, tensors), out_shape=jax....]
    unnamed x15 -> x1, local copies, waits for them, and re-layouts: 14.6 us -> 1.35 us
    dot_general x7 -> x0, matrix products: 7.71 us -> none  [the longest x1 1.71 us: on_device(): jnp.dot(low_rank_output, up_whole.astype(jnp.float32), precision=lax.Prec...]
  transfers between devices with their start and end apart: 4 -> 0, of which waited for: 4 -> 0; matrix products, arithmetic and copies ran while one was open for 2% -> 0% of each run, Pallas kernels for 0% -> 0%
where the time goes in v1:
time: 35.3 us; the launch traced here: 35.1 us
  Pallas kernels  33.7 us (95%)
  local copies, waits for them, and re-layouts  1.35 us (4%)
    pallas_call x1, Pallas kernels, on_device(): pl.pallas_call(functools.partial(kernel, groups, tensors), out_shape=jax....  33.7 us
    unnamed x1, local copies, waits for them, and re-layouts  1.35 us

profile of v1, /device:TPU:1, one launch (start us, length us, event | category | flops | bytes accessed | tf_op | source)
XLA Modules:
  0.0 35.1 jit_solution(212420860748308129)
XLA Ops:
  0.0 33.7 %shard_map.91 = bf16[4,8,320]{2,1,0:T(8,128)(2,1)} custom-call(bf16[4,8,256]{2,1,0:T(8,128)(2,1)} %q_hbm.1, bf16[8,512,128]{2,1,0:T(8,128)(2,1)} %bitcast.6, bf16[8,512,128]{2,1,0:T(8,128)(2,1)} %bitcast.7, bf16[4,8,128]{2,1,0:T(8,128)(2,1)} %bitcast.8, bf16[4,8,128]{2,1,0:T(8,128)(2,1)} %bitcast.9, s32[1,8]{1,0:T(1,128)} %bitcast.11, ...), custom_call_target="tpu_custom_call" | custom-call | tf_op jit(solution)/shard_map/pallas_call | solution.py:277
  33.8 1.3 %copy.11 = bf16[4,8,320]{2,1,0:T(8,128)(2,1)} copy(bf16[4,8,320]{2,1,0:T(8,128)(2,1)} %shard_map.91) | data formatting | bytes 40960

commit v2 on v1

--- a/solution.py
+++ b/solution.py
@@ -43,7 +43,9 @@
     down_v,
     up_v,
     gath,
-    factors,
+    down_f,
+    up_f,
+    lows,
     keep,
     send1,
     recv1,
@@ -53,8 +55,12 @@
     k_sem,
     v_sem,
     w_sem,
-    gsend_sem,
-    grecv_sem,
+    met_sem,
+    mine_sem,
+    gath_sent,
+    gath_sem,
+    low_sent,
+    low_sem,
     s1_sem,
     r1_sem,
     s2_sem,
@@ -64,21 +70,22 @@
     cache = k_v.shape[0]
     toks = steps * rows
     cols = out_ref.shape[2]
-    depth = down_v.shape[1]
     chips = tensors // 2
-    rank = factors.shape[0]
+    rank = down_f.shape[0]
 
     g = lax.axis_index("group")
     t = lax.axis_index("tensor")
     chip = t // 2
     core = t % 2
+    planes = groups // 2
+    z = lax.rem(g, planes)
+    order = 2 * z + g // planes
+    late = (2 * z) // planes
 
     smalls = [
         pltpu.make_async_copy(src, dst, small_sem.at[i])
         for i, (src, dst) in enumerate(
             [
-                (down_hbm, down_v),
-                (up_hbm, up_v),
                 (q_hbm, q_v),
                 (sk_hbm, sk_v),
                 (sv_hbm, sv_v),
@@ -86,8 +93,6 @@
             ]
         )
     ]
-    for c in smalls:
-        c.start()
     k_copies = [
         pltpu.make_async_copy(k_hbm.at[r], k_v.at[:, pl.ds(r * HEAD_SIZE, HEAD_SIZE)], k_sem.at[r])
         for r in range(rows)
@@ -107,47 +112,87 @@
         )
         for k in range(chips)
     ]
-    for c in k_copies + v_copies + w_copies:
+    mine_copies = [
+        pltpu.make_async_copy(down_hbm, down_v, mine_sem.at[0]),
+        pltpu.make_async_copy(up_hbm, up_v, mine_sem.at[1]),
+    ]
+    for c in mine_copies + smalls + k_copies + v_copies + w_copies:
         c.start()
 
     barrier = pltpu.get_barrier_semaphore()
-
-    def greet_group(d, carry):
+    home = t - core
+    partner = {"tensor": home + 1 - core}
+
+    def group_at(k):
+        return lax.rem(k, 2) * planes + k // 2
+
+    def greet_group(k, carry):
         pl.semaphore_signal(
-            barrier, inc=1, device_id={"group": lax.rem(g + d, groups)}, device_id_type=MESH
+            barrier,
+            inc=1,
+            device_id={"group": group_at(k), "tensor": home + late},
+            device_id_type=MESH,
         )
         return carry
 
-    lax.fori_loop(1, groups, greet_group, 0)
-    pl.semaphore_signal(barrier, inc=1, device_id={"tensor": t + 1 - 2 * core}, device_id_type=MESH)
+    lax.fori_loop(0, order, greet_group, 0)
+    lax.fori_loop(order + 1, groups, greet_group, 0)
     for k in range(chips - 1):
         pl.semaphore_signal(
-            barrier, inc=1, device_id={"tensor": chunk_at(k) * 2 + core}, device_id_type=MESH
-        )
-    own = groups - 1
-    smalls[0].wait()
-    smalls[1].wait()
-    gath[own, :, 0:depth] = down_v[...]
-    gath[own, :, depth : depth + cols] = up_v[...]
-    gath[own, :, depth + cols :] = jnp.zeros(
+            barrier, inc=1, device_id={"tensor": chunk_at(k) * 2 + late}, device_id_type=MESH
+        )
+
+    @pl.when(core == 1)
+    def _():
+        pl.semaphore_signal(barrier, inc=1, device_id=partner, device_id_type=MESH)
+
+    for c in mine_copies:
+        c.wait()
+    depth = down_v.shape[1]
+    gath[order, :, 0:depth] = down_v[...]
+    gath[order, :, depth : depth + cols] = up_v[...]
+    gath[order, :, depth + cols :] = jnp.zeros(
         (gath.shape[1], gath.shape[2] - depth - cols), gath.dtype
     )
-    pl.semaphore_wait(barrier, (groups - 1) + 1 + (chips - 1))
-
-    def send_factors(d, carry):
+
+    def send_factors(k, carry):
         pltpu.make_async_remote_copy(
-            src_ref=gath.at[own],
-            dst_ref=gath.at[d],
-            send_sem=gsend_sem,
-            recv_sem=grecv_sem,
-            device_id={"group": lax.rem(g + d + 1, groups)},
+            src_ref=gath.at[order],
+            dst_ref=gath.at[order],
+            send_sem=gath_sent,
+            recv_sem=gath_sem,
+            device_id={"group": group_at(k)},
             device_id_type=MESH,
         ).start()
         return carry
 
-    lax.fori_loop(0, groups - 1, send_factors, 0)
-
-    for c in smalls[2:]:
+    half = groups // 2
+
+    def meet(mail, count, first):
+        @pl.when(core == mail)
+        def _():
+            pl.semaphore_wait(barrier, count)
+            pl.semaphore_signal(met_sem.at[mail], inc=1, device_id=partner, device_id_type=MESH)
+
+        @pl.when(core != mail)
+        def _():
+            pl.semaphore_wait(met_sem.at[mail], 1)
+
+        lax.fori_loop(first, jnp.clip(order, first, first + half), send_factors, 0)
+        lax.fori_loop(jnp.clip(order + 1, first, first + half), first + half, send_factors, 0)
+
+    plane = 2 * (chips - 1)
+
+    def meet_first():
+        meet(0, 2 * half + 1 + (1 - late) * (plane - 2), 0)
+
+    def meet_second():
+        meet(1, 2 * half + late * (plane - 2), half)
+
+    hurry = 4 * z >= planes
+    pl.when(hurry)(meet_first)
+
+    for c in smalls:
         c.wait()
     q32 = jnp.concatenate([q_v[s].astype(jnp.float32) for s in range(steps)], axis=0)
     q64 = jnp.concatenate([q32[:, h * HEAD_SIZE : (h + 1) * HEAD_SIZE] for h in range(QH)], axis=0)
@@ -195,22 +240,18 @@
     attended = jnp.concatenate([mixed[h * toks : (h + 1) * toks] for h in range(QH)], axis=1)
     attended = attended.astype(jnp.bfloat16)
 
-    others = gath.at[pl.ds(0, groups - 1)]
-    pltpu.make_async_copy(others, others, grecv_sem).wait()
-    per = gath.shape[1]
-    for i in range(groups):
-        factors[per * i : per * (i + 1), :] = gath[i].astype(jnp.float32)
-    low = nt_dot(attended, factors[:, 0:depth].astype(jnp.bfloat16))
-
-    to_partner = []
     for k in range(chips):
         w_copies[k].wait()
         part = jnp.dot(attended, w_v[k], preferred_element_type=jnp.float32)
         first, second = part[:, :cols], part[:, cols:]
-        mine = jnp.where(core == 0, first, second)
-        theirs = jnp.where(core == 0, second, first)
-        keep[k, :, :] = jnp.concatenate([mine, low], axis=1)
-        send1[k, :, :] = jnp.concatenate([theirs, low], axis=1).astype(jnp.bfloat16)
+        keep[k, :, :] = jnp.where(core == 0, first, second)
+        send1[k, :, :] = jnp.where(core == 0, second, first).astype(jnp.bfloat16)
+
+    pl.when(jnp.logical_not(hurry))(meet_first)
+    pl.when(late == 1)(meet_second)
+
+    to_partner = []
+    for k in range(chips):
         copy = pltpu.make_async_remote_copy(
             src_ref=send1.at[k],
             dst_ref=recv1.at[k],
@@ -241,21 +282,57 @@
         else:
             total = both
 
-    up = factors[:, depth : depth + cols].astype(jnp.bfloat16)
+    pl.when(late == 0)(meet_second)
+    others = gath.at[pl.ds(0, groups - 1)]
+    pltpu.make_async_copy(others, others, gath_sem).wait()
+
+    per = gath.shape[1]
+    for i in range(groups):
+        down_f[per * i : per * (i + 1), :] = gath[i, :, 0:depth].astype(jnp.float32)
+    low = nt_dot(attended, down_f[...].astype(jnp.bfloat16))
+    top_rows = toks // 2
+    low = jnp.concatenate([low[:top_rows], low[top_rows:]], axis=1)
+    lows[tensors - 1, :, :] = low.astype(jnp.bfloat16)
+    low_copies = [
+        pltpu.make_async_remote_copy(
+            src_ref=lows.at[tensors - 1],
+            dst_ref=lows.at[d],
+            send_sem=low_sent,
+            recv_sem=low_sem,
+            device_id={"tensor": lax.rem(t + d + 1, tensors)},
+            device_id_type=MESH,
+        )
+        for d in range(tensors - 1)
+    ]
+    for copy in low_copies:
+        copy.start()
+
+    for i in range(groups):
+        up_f[per * i : per * (i + 1), :] = gath[i, :, depth : depth + cols].astype(jnp.float32)
+    up = up_f[...].astype(jnp.bfloat16)
+    up = jnp.concatenate([up, up], axis=0)
     for k in range(chips - 1):
         to_chips[k].wait_recv()
         total = total + recv2[k].astype(jnp.float32)
-    low = total[:, cols : cols + rank]
+    others = lows.at[pl.ds(0, tensors - 1)]
+    pltpu.make_async_copy(others, others, low_sem).wait()
+    low = lows[0].astype(jnp.float32)
+    for d in range(1, tensors):
+        low = low + lows[d].astype(jnp.float32)
+    left = lax.broadcasted_iota(jnp.int32, low.shape, 1) < rank
+    low = jnp.concatenate([jnp.where(left, low, 0.0), jnp.where(left, 0.0, low)], axis=0)
     high = low.astype(jnp.bfloat16)
     rest = (low - high.astype(jnp.float32)).astype(jnp.bfloat16)
     delta = jnp.dot(high, up, preferred_element_type=jnp.float32) + jnp.dot(
         rest, up, preferred_element_type=jnp.float32
     )
-    result = (total[:, :cols] + 2.0 * delta).astype(out_ref.dtype)
+    result = (total + 2.0 * delta).astype(out_ref.dtype)
     for s in range(steps):
         out_ref[s, :, :] = result[s * rows : (s + 1) * rows]
 
-    pltpu.make_async_copy(others, others, gsend_sem).wait()
+    pltpu.make_async_copy(others, others, low_sent).wait()
+    others = gath.at[pl.ds(0, groups - 1)]
+    pltpu.make_async_copy(others, others, gath_sent).wait()
     for copy in to_partner + to_chips:
         copy.wait_send()
 
@@ -269,7 +346,6 @@
     chips = tensors // 2
     toks = steps * rows
     rank = per * groups
-    chunk = cols + rank
     message = -(-(depth + cols) // 128) * 128
     bf16, f32 = jnp.bfloat16, jnp.float32
     hbm = pl.BlockSpec(memory_space=pltpu.HBM)
@@ -290,16 +366,22 @@
             pltpu.VMEM((per, depth), bf16),
             pltpu.VMEM((per, cols), bf16),
             pltpu.VMEM((groups, per, message), bf16),
-            pltpu.VMEM((rank, message), f32),
-            pltpu.VMEM((chips, toks, chunk), f32),
-            pltpu.VMEM((chips, toks, chunk), bf16),
-            pltpu.VMEM((chips, toks, chunk), bf16),
-            pltpu.VMEM((chips - 1, toks, chunk), bf16),
-            pltpu.VMEM((chips - 1, toks, chunk), bf16),
-            dma((6,)),
+            pltpu.VMEM((rank, depth), f32),
+            pltpu.VMEM((rank, cols), f32),
+            pltpu.VMEM((tensors, toks // 2, 2 * rank), bf16),
+            pltpu.VMEM((chips, toks, cols), f32),
+            pltpu.VMEM((chips, toks, cols), bf16),
+            pltpu.VMEM((chips, toks, cols), bf16),
+            pltpu.VMEM((chips - 1, toks, cols), bf16),
+            pltpu.VMEM((chips - 1, toks, cols), bf16),
+            dma((4,)),
             dma((rows,)),
             dma((rows,)),
             dma((chips,)),
+            pltpu.SemaphoreType.REGULAR((2,)),
+            dma((2,)),
+            dma,
+            dma,
             dma,
             dma,
             dma((chips,)),

time: 35.3 us -> 30.6 us (0.87)
  Pallas kernels: 33.7 us -> 29 us
    pallas_call x1, Pallas kernels: 33.7 us -> 29 us  [on_device(): pl.pallas_call(functools.partial(kernel, groups, tensors), out_shape=jax....]
where the time goes in v2:
time: 30.6 us; the launch traced here: 30.4 us
  Pallas kernels  29 us (95%)
  local copies, waits for them, and re-layouts  1.35 us (4%)
    pallas_call x1, Pallas kernels, on_device(): pl.pallas_call(functools.partial(kernel, groups, tensors), out_shape=jax....  29 us
    unnamed x1, local copies, waits for them, and re-layouts  1.35 us

profile of v2, /device:TPU:1, one launch (start us, length us, event | category | flops | bytes accessed | tf_op | source)
XLA Modules:
  0.0 30.4 jit_solution(6478162298676096000)
XLA Ops:
  0.0 29.0 %shard_map.91 = bf16[4,8,320]{2,1,0:T(8,128)(2,1)} custom-call(bf16[4,8,256]{2,1,0:T(8,128)(2,1)} %q_hbm.1, bf16[8,512,128]{2,1,0:T(8,128)(2,1)} %bitcast.6, bf16[8,512,128]{2,1,0:T(8,128)(2,1)} %bitcast.7, bf16[4,8,128]{2,1,0:T(8,128)(2,1)} %bitcast.8, bf16[4,8,128]{2,1,0:T(8,128)(2,1)} %bitcast.9, s32[1,8]{1,0:T(1,128)} %bitcast.11, ...), custom_call_target="tpu_custom_call" | custom-call | tf_op jit(solution)/shard_map/pallas_call | solution.py:353
  29.0 1.3 %copy.11 = bf16[4,8,320]{2,1,0:T(8,128)(2,1)} copy(bf16[4,8,320]{2,1,0:T(8,128)(2,1)} %shard_map.91) | data formatting | bytes 40960

commit v3 on v2

--- a/solution.py
+++ b/solution.py
@@ -42,7 +42,8 @@
     w_v,
     down_v,
     up_v,
-    gath,
+    gdown,
+    gup,
     down_f,
     up_f,
     lows,
@@ -57,8 +58,8 @@
     w_sem,
     met_sem,
     mine_sem,
-    gath_sent,
-    gath_sem,
+    sent_sem,
+    come_sem,
     low_sent,
     low_sem,
     s1_sem,
@@ -116,81 +117,95 @@
         pltpu.make_async_copy(down_hbm, down_v, mine_sem.at[0]),
         pltpu.make_async_copy(up_hbm, up_v, mine_sem.at[1]),
     ]
-    for c in mine_copies + smalls + k_copies + v_copies + w_copies:
+    for c in mine_copies:
         c.start()
+
+    def start_loads():
+        for c in smalls + k_copies + v_copies + w_copies:
+            c.start()
+
 
     barrier = pltpu.get_barrier_semaphore()
     home = t - core
     partner = {"tensor": home + 1 - core}
+    half = groups // 2
+    first_mail = 0
+    plane = 2 * (chips - 1)
+
+    @pl.when(core != first_mail)
+    def _():
+        pl.semaphore_signal(barrier, inc=1, device_id=partner, device_id_type=MESH)
 
     def group_at(k):
         return lax.rem(k, 2) * planes + k // 2
 
-    def greet_group(k, carry):
-        pl.semaphore_signal(
-            barrier,
-            inc=1,
-            device_id={"group": group_at(k), "tensor": home + late},
-            device_id_type=MESH,
-        )
-        return carry
-
-    lax.fori_loop(0, order, greet_group, 0)
-    lax.fori_loop(order + 1, groups, greet_group, 0)
-    for k in range(chips - 1):
-        pl.semaphore_signal(
-            barrier, inc=1, device_id={"tensor": chunk_at(k) * 2 + late}, device_id_type=MESH
-        )
-
-    @pl.when(core == 1)
-    def _():
-        pl.semaphore_signal(barrier, inc=1, device_id=partner, device_id_type=MESH)
-
-    for c in mine_copies:
-        c.wait()
-    depth = down_v.shape[1]
-    gath[order, :, 0:depth] = down_v[...]
-    gath[order, :, depth : depth + cols] = up_v[...]
-    gath[order, :, depth + cols :] = jnp.zeros(
-        (gath.shape[1], gath.shape[2] - depth - cols), gath.dtype
-    )
-
-    def send_factors(k, carry):
-        pltpu.make_async_remote_copy(
-            src_ref=gath.at[order],
-            dst_ref=gath.at[order],
-            send_sem=gath_sent,
-            recv_sem=gath_sem,
-            device_id={"group": group_at(k)},
-            device_id_type=MESH,
-        ).start()
-        return carry
-
-    half = groups // 2
-
-    def meet(mail, count, first):
+    def greet():
+        def greet_group(i, carry):
+            away = (i + 1) // 2 * (1 - 2 * lax.rem(i, 2))
+            k = lax.rem(order + half + away + groups, groups)
+            there = k // half
+            mail = late
+            pl.semaphore_signal(
+                barrier,
+                inc=1,
+                device_id={"group": group_at(k), "tensor": home + mail},
+                device_id_type=MESH,
+            )
+            return carry
+
+        lax.fori_loop(0, groups - 1, greet_group, 0)
+        for k in range(chips - 1):
+            pl.semaphore_signal(
+                barrier, inc=1, device_id={"tensor": chunk_at(k) * 2 + late}, device_id_type=MESH
+            )
+
+    def meet(which, mail, count):
         @pl.when(core == mail)
         def _():
             pl.semaphore_wait(barrier, count)
-            pl.semaphore_signal(met_sem.at[mail], inc=1, device_id=partner, device_id_type=MESH)
+            pl.semaphore_signal(met_sem.at[which], inc=1, device_id=partner, device_id_type=MESH)
 
         @pl.when(core != mail)
         def _():
-            pl.semaphore_wait(met_sem.at[mail], 1)
-
-        lax.fori_loop(first, jnp.clip(order, first, first + half), send_factors, 0)
-        lax.fori_loop(jnp.clip(order + 1, first, first + half), first + half, send_factors, 0)
-
-    plane = 2 * (chips - 1)
+            pl.semaphore_wait(met_sem.at[which], 1)
 
     def meet_first():
-        meet(0, 2 * half + 1 + (1 - late) * (plane - 2), 0)
+        meet(0, first_mail, 2 * half + 1 + (1 - late) * (plane - 2))
 
     def meet_second():
-        meet(1, 2 * half + late * (plane - 2), half)
+        meet(1, 1 - first_mail, 2 * half + late * (plane - 2))
+
+    def send_to(first, which):
+        src, dst = ((down_v, gdown), (up_v, gup))[which]
+
+        def send(k, carry):
+            pltpu.make_async_remote_copy(
+                src_ref=src,
+                dst_ref=dst.at[order],
+                send_sem=sent_sem.at[which],
+                recv_sem=come_sem.at[which],
+                device_id={"group": group_at(k)},
+                device_id_type=MESH,
+            ).start()
+            return carry
+
+        lax.fori_loop(first, jnp.clip(order, first, first + half), send, 0)
+        lax.fori_loop(jnp.clip(order + 1, first, first + half), first + half, send, 0)
+
+    def wait_mine():
+        for c in mine_copies:
+            c.wait()
 
     hurry = 4 * z >= planes
-    pl.when(hurry)(meet_first)
+
+    greet()
+    start_loads()
+    wait_mine()
+
+    @pl.when(hurry)
+    def _():
+        meet_first()
+        send_to(0, 0)
 
     for c in smalls:
         c.wait()
@@ -240,6 +255,8 @@
     attended = jnp.concatenate([mixed[h * toks : (h + 1) * toks] for h in range(QH)], axis=1)
     attended = attended.astype(jnp.bfloat16)
 
+    pl.when(hurry)(lambda: send_to(0, 1))
+
     for k in range(chips):
         w_copies[k].wait()
         part = jnp.dot(attended, w_v[k], preferred_element_type=jnp.float32)
@@ -247,8 +264,17 @@
         keep[k, :, :] = jnp.where(core == 0, first, second)
         send1[k, :, :] = jnp.where(core == 0, second, first).astype(jnp.bfloat16)
 
-    pl.when(jnp.logical_not(hurry))(meet_first)
-    pl.when(late == 1)(meet_second)
+    @pl.when(jnp.logical_not(hurry))
+    def _():
+        meet_first()
+        send_to(0, 0)
+        send_to(0, 1)
+
+    @pl.when(late == 1)
+    def _():
+        meet_second()
+        send_to(half, 0)
+
 
     to_partner = []
     for k in range(chips):
@@ -282,13 +308,20 @@
         else:
             total = both
 
-    pl.when(late == 0)(meet_second)
-    others = gath.at[pl.ds(0, groups - 1)]
-    pltpu.make_async_copy(others, others, gath_sem).wait()
-
-    per = gath.shape[1]
+    @pl.when(late == 0)
+    def _():
+        meet_second()
+        send_to(half, 0)
+
+    gdown[order] = down_v[...]
+    gup[order] = up_v[...]
+    downs = gdown.at[pl.ds(0, groups - 1)]
+    ups = gup.at[pl.ds(0, groups - 1)]
+    pltpu.make_async_copy(downs, downs, come_sem.at[0]).wait()
+
+    per = gdown.shape[1]
     for i in range(groups):
-        down_f[per * i : per * (i + 1), :] = gath[i, :, 0:depth].astype(jnp.float32)
+        down_f[per * i : per * (i + 1), :] = gdown[i].astype(jnp.float32)
     low = nt_dot(attended, down_f[...].astype(jnp.bfloat16))
     top_rows = toks // 2
     low = jnp.concatenate([low[:top_rows], low[top_rows:]], axis=1)
@@ -307,8 +340,10 @@
     for copy in low_copies:
         copy.start()
 
+    send_to(half, 1)
+    pltpu.make_async_copy(ups, ups, come_sem.at[1]).wait()
     for i in range(groups):
-        up_f[per * i : per * (i + 1), :] = gath[i, :, depth : depth + cols].astype(jnp.float32)
+        up_f[per * i : per * (i + 1), :] = gup[i].astype(jnp.float32)
     up = up_f[...].astype(jnp.bfloat16)
     up = jnp.concatenate([up, up], axis=0)
     for k in range(chips - 1):
@@ -331,8 +366,8 @@
         out_ref[s, :, :] = result[s * rows : (s + 1) * rows]
 
     pltpu.make_async_copy(others, others, low_sent).wait()
-    others = gath.at[pl.ds(0, groups - 1)]
-    pltpu.make_async_copy(others, others, gath_sent).wait()
+    pltpu.make_async_copy(downs, downs, sent_sem.at[0]).wait()
+    pltpu.make_async_copy(ups, ups, sent_sem.at[1]).wait()
     for copy in to_partner + to_chips:
         copy.wait_send()
 
@@ -346,13 +381,12 @@
     chips = tensors // 2
     toks = steps * rows
     rank = per * groups
-    message = -(-(depth + cols) // 128) * 128
     bf16, f32 = jnp.bfloat16, jnp.float32
     hbm = pl.BlockSpec(memory_space=pltpu.HBM)
     dma = pltpu.SemaphoreType.DMA
     return pl.pallas_call(
         functools.partial(kernel, groups, tensors),
-        out_shape=jax.ShapeDtypeStruct((steps, rows, cols), bf16),
+        out_shape=pltpu.VMEM((steps, rows, cols), bf16),
         in_specs=[hbm] * 9,
         out_specs=pl.BlockSpec(memory_space=pltpu.VMEM),
         scratch_shapes=[
@@ -365,7 +399,8 @@
             pltpu.VMEM((chips, depth, 2 * cols), bf16),
             pltpu.VMEM((per, depth), bf16),
             pltpu.VMEM((per, cols), bf16),
-            pltpu.VMEM((groups, per, message), bf16),
+            pltpu.VMEM((groups, per, depth), bf16),
+            pltpu.VMEM((groups, per, cols), bf16),
             pltpu.VMEM((rank, depth), f32),
             pltpu.VMEM((rank, cols), f32),
             pltpu.VMEM((tensors, toks // 2, 2 * rank), bf16),
@@ -380,8 +415,8 @@
             dma((chips,)),
             pltpu.SemaphoreType.REGULAR((2,)),
             dma((2,)),
-            dma,
-            dma,
+            dma((2,)),
+            dma((2,)),
             dma,
             dma,
             dma((chips,)),

time: 30.6 us -> 28.5 us (0.931)
  Pallas kernels: 29 us -> 27.7 us
  local copies, waits for them, and re-layouts: 1.35 us -> 0.61 us
    pallas_call x1, Pallas kernels: 29 us -> 27.7 us  [on_device(): pl.pallas_call(functools.partial(kernel, groups, tensors), out_shape=pltp...]
    unnamed x1, local copies, waits for them, and re-layouts: 1.35 us -> 0.61 us
where the time goes in v3:
time: 28.5 us; the launch traced here: 28.4 us
  Pallas kernels  27.7 us (97%)
  local copies, waits for them, and re-layouts  0.61 us (2%)
    pallas_call x1, Pallas kernels, on_device(): pl.pallas_call(functools.partial(kernel, groups, tensors), out_shape=pltp...  27.7 us
    unnamed x1, local copies, waits for them, and re-layouts  0.61 us

profile of v3, /device:TPU:1, one launch (start us, length us, event | category | flops | bytes accessed | tf_op | source)
XLA Modules:
  0.0 28.4 jit_solution(14746613926439271857)
XLA Ops:
  0.0 27.7 %shard_map.91 = bf16[4,8,320]{2,1,0:T(8,128)(2,1)S(1)} custom-call(bf16[4,8,256]{2,1,0:T(8,128)(2,1)} %q_hbm.1, bf16[8,512,128]{2,1,0:T(8,128)(2,1)} %bitcast.6, bf16[8,512,128]{2,1,0:T(8,128)(2,1)} %bitcast.7, bf16[4,8,128]{2,1,0:T(8,128)(2,1)} %bitcast.8, bf16[4,8,128]{2,1,0:T(8,128)(2,1)} %bitcast.9, s32[1,8]{1,0:T(1,128)} %bitcast.11, ...), custom_call_target="tpu_custom_call" | custom-call | tf_op jit(solution)/shard_map/pallas_call | solution.py:387
  27.7 0.6 %copy.11 = bf16[4,8,320]{2,1,0:T(8,128)(2,1)} copy(bf16[4,8,320]{2,1,0:T(8,128)(2,1)S(1)} %shard_map.91) | data formatting | bytes 40960

commit v4 on v3

--- a/solution.py
+++ b/solution.py
@@ -99,19 +99,18 @@
         for r in range(rows)
     ]
     v_copies = [
-        pltpu.make_async_copy(v_hbm.at[r], v_v.at[pl.ds(r * cache, cache)], v_sem.at[r])
-        for r in range(rows)
+        pltpu.make_async_copy(v_hbm.at[part], v_v.at[part], v_sem.at[i])
+        for i, part in enumerate((pl.ds(0, rows // 2), pl.ds(rows // 2, rows // 2)))
     ]
     pair = 2 * cols
 
     def chunk_at(k):
         return lax.rem(chip + k + 1, chips)
 
+    depth = w_v.shape[0]
     w_copies = [
-        pltpu.make_async_copy(
-            w_hbm.at[:, pl.ds(pl.multiple_of(chunk_at(k) * pair, 128), pair)], w_v.at[k], w_sem.at[k]
-        )
-        for k in range(chips)
+        pltpu.make_async_copy(w_hbm.at[part], w_v.at[part], w_sem.at[i])
+        for i, part in enumerate(pl.ds(i * (depth // 4), depth // 4) for i in range(4))
     ]
     mine_copies = [
         pltpu.make_async_copy(down_hbm, down_v, mine_sem.at[0]),
@@ -119,17 +118,13 @@
     ]
     for c in mine_copies:
         c.start()
-
-    def start_loads():
-        for c in smalls + k_copies + v_copies + w_copies:
-            c.start()
 
 
     barrier = pltpu.get_barrier_semaphore()
     home = t - core
     partner = {"tensor": home + 1 - core}
     half = groups // 2
-    first_mail = 0
+    first_mail = late
     plane = 2 * (chips - 1)
 
     @pl.when(core != first_mail)
@@ -144,7 +139,7 @@
             away = (i + 1) // 2 * (1 - 2 * lax.rem(i, 2))
             k = lax.rem(order + half + away + groups, groups)
             there = k // half
-            mail = late
+            mail = late + there - 2 * late * there
             pl.semaphore_signal(
                 barrier,
                 inc=1,
@@ -156,7 +151,7 @@
         lax.fori_loop(0, groups - 1, greet_group, 0)
         for k in range(chips - 1):
             pl.semaphore_signal(
-                barrier, inc=1, device_id={"tensor": chunk_at(k) * 2 + late}, device_id_type=MESH
+                barrier, inc=1, device_id={"tensor": chunk_at(k) * 2}, device_id_type=MESH
             )
 
     def meet(which, mail, count):
@@ -183,7 +178,7 @@
                 src_ref=src,
                 dst_ref=dst.at[order],
                 send_sem=sent_sem.at[which],
-                recv_sem=come_sem.at[which],
+                recv_sem=come_sem.at[which, late],
                 device_id={"group": group_at(k)},
                 device_id_type=MESH,
             ).start()
@@ -198,14 +193,21 @@
 
     hurry = 4 * z >= planes
 
-    greet()
-    start_loads()
+    last = (late == 1) & (4 * z < 3 * planes)
+    pl.when(jnp.logical_not(last))(greet)
+    for c in smalls + k_copies:
+        c.start()
     wait_mine()
 
     @pl.when(hurry)
     def _():
         meet_first()
         send_to(0, 0)
+
+    pl.when(last)(greet)
+
+    for c in v_copies + w_copies:
+        c.start()
 
     for c in smalls:
         c.wait()
@@ -251,15 +253,24 @@
     weights = jnp.concatenate(
         [jnp.where(row_of == r, cached, 0.0).astype(jnp.bfloat16) for r in range(rows)], axis=1
     )
-    mixed = mixed + jnp.dot(weights, v_v[...], preferred_element_type=jnp.float32)
+    mixed = mixed + jnp.dot(
+        weights, v_v[...].reshape(rows * cache, HEAD_SIZE), preferred_element_type=jnp.float32)
     attended = jnp.concatenate([mixed[h * toks : (h + 1) * toks] for h in range(QH)], axis=1)
     attended = attended.astype(jnp.bfloat16)
 
     pl.when(hurry)(lambda: send_to(0, 1))
 
+    @pl.when(late == 1)
+    def _():
+        meet_second()
+        send_to(half, 0)
+
+    for c in w_copies:
+        c.wait()
     for k in range(chips):
-        w_copies[k].wait()
-        part = jnp.dot(attended, w_v[k], preferred_element_type=jnp.float32)
+        part = jnp.dot(
+            attended, w_v[:, k * pair : (k + 1) * pair], preferred_element_type=jnp.float32
+        )
         first, second = part[:, :cols], part[:, cols:]
         keep[k, :, :] = jnp.where(core == 0, first, second)
         send1[k, :, :] = jnp.where(core == 0, second, first).astype(jnp.bfloat16)
@@ -270,16 +281,11 @@
         send_to(0, 0)
         send_to(0, 1)
 
-    @pl.when(late == 1)
-    def _():
-        meet_second()
-        send_to(half, 0)
-
 
     to_partner = []
     for k in range(chips):
         copy = pltpu.make_async_remote_copy(
-            src_ref=send1.at[k],
+            src_ref=send1.at[chunk_at(k)],
             dst_ref=recv1.at[k],
             send_sem=s1_sem.at[k],
             recv_sem=r1_sem.at[k],
@@ -292,7 +298,7 @@
     to_chips = []
     for k in range(chips):
         to_partner[k].wait_recv()
-        both = keep[k] + recv1[k].astype(jnp.float32)
+        both = keep[chunk_at(k)] + recv1[k].astype(jnp.float32)
         if k < chips - 1:
             send2[k, :, :] = both.astype(jnp.bfloat16)
             copy = pltpu.make_async_remote_copy(
@@ -317,31 +323,53 @@
     gup[order] = up_v[...]
     downs = gdown.at[pl.ds(0, groups - 1)]
     ups = gup.at[pl.ds(0, groups - 1)]
-    pltpu.make_async_copy(downs, downs, come_sem.at[0]).wait()
+
+    def wait_half(which, buffer, h):
+        for mine in (0, 1):
+            blocks = buffer.at[pl.ds(0, half - mine)]
+
+            @pl.when((late == h) == (mine == 1))
+            def _():
+                pltpu.make_async_copy(blocks, blocks, come_sem.at[which, h]).wait()
+
 
     per = gdown.shape[1]
-    for i in range(groups):
-        down_f[per * i : per * (i + 1), :] = gdown[i].astype(jnp.float32)
+    for h in range(2):
+        wait_half(0, gdown, h)
+        for i in range(h * half, (h + 1) * half):
+            down_f[per * i : per * (i + 1), :] = gdown[i].astype(jnp.float32)
     low = nt_dot(attended, down_f[...].astype(jnp.bfloat16))
     top_rows = toks // 2
     low = jnp.concatenate([low[:top_rows], low[top_rows:]], axis=1)
     lows[tensors - 1, :, :] = low.astype(jnp.bfloat16)
+    xs = chips // 2
+    steps_away = sorted(
+        ((a, b, c) for a in range(2) for b in range(xs) for c in range(2) if a + b + c),
+        key=lambda s: (-2 * s[0] - min(s[1], xs - s[1]), s[2]),
+    )
+    far_first = [
+        lax.rem(t // (2 * xs) + a, 2) * 2 * xs
+        + lax.rem(lax.rem(chip, xs) + b, xs) * 2
+        + lax.rem(core + c, 2)
+        for a, b, c in steps_away
+    ]
     low_copies = [
         pltpu.make_async_remote_copy(
             src_ref=lows.at[tensors - 1],
             dst_ref=lows.at[d],
             send_sem=low_sent,
             recv_sem=low_sem,
-            device_id={"tensor": lax.rem(t + d + 1, tensors)},
+            device_id={"tensor": other},
             device_id_type=MESH,
         )
-        for d in range(tensors - 1)
+        for d, other in enumerate(far_first)
     ]
     for copy in low_copies:
         copy.start()
 
     send_to(half, 1)
-    pltpu.make_async_copy(ups, ups, come_sem.at[1]).wait()
+    for h in range(2):
+        wait_half(1, gup, h)
     for i in range(groups):
         up_f[per * i : per * (i + 1), :] = gup[i].astype(jnp.float32)
     up = up_f[...].astype(jnp.bfloat16)
@@ -392,11 +420,11 @@
         scratch_shapes=[
             pltpu.VMEM((steps, rows, width), bf16),
             pltpu.VMEM((cache, rows * HEAD_SIZE), bf16),
-            pltpu.VMEM((rows * cache, HEAD_SIZE), bf16),
+            pltpu.VMEM((rows, cache, HEAD_SIZE), bf16),
             pltpu.VMEM((steps, rows, HEAD_SIZE), bf16),
             pltpu.VMEM((steps, rows, HEAD_SIZE), bf16),
             pltpu.VMEM((1, rows), jnp.int32),
-            pltpu.VMEM((chips, depth, 2 * cols), bf16),
+            pltpu.VMEM((depth, weight.shape[1]), bf16),
             pltpu.VMEM((per, depth), bf16),
             pltpu.VMEM((per, cols), bf16),
             pltpu.VMEM((groups, per, depth), bf16),
@@ -411,12 +439,12 @@
             pltpu.VMEM((chips - 1, toks, cols), bf16),
             dma((4,)),
             dma((rows,)),
-            dma((rows,)),
-            dma((chips,)),
+            dma((2,)),
+            dma((4,)),
             pltpu.SemaphoreType.REGULAR((2,)),
             dma((2,)),
             dma((2,)),
-            dma((2,)),
+            dma((2, 2)),
             dma,
             dma,
             dma((chips,)),

time: 28.5 us -> 28.3 us (level)
  no operation moved by 1% of the time
where the time goes in v4:
time: 28.3 us; the launch traced here: 28.2 us
  Pallas kernels  27.6 us (98%)
  local copies, waits for them, and re-layouts  0.61 us (2%)
    pallas_call x1, Pallas kernels, on_device(): pl.pallas_call(functools.partial(kernel, groups, tensors), out_shape=pltp...  27.6 us
    unnamed x1, local copies, waits for them, and re-layouts  0.61 us

profile of v4, /device:TPU:1, one launch (start us, length us, event | category | flops | bytes accessed | tf_op | source)
XLA Modules:
  0.0 28.2 jit_solution(2374291590700763936)
XLA Ops:
  0.0 27.6 %shard_map.91 = bf16[4,8,320]{2,1,0:T(8,128)(2,1)S(1)} custom-call(bf16[4,8,256]{2,1,0:T(8,128)(2,1)} %q_hbm.1, bf16[8,512,128]{2,1,0:T(8,128)(2,1)} %bitcast.6, bf16[8,512,128]{2,1,0:T(8,128)(2,1)} %bitcast.7, bf16[4,8,128]{2,1,0:T(8,128)(2,1)} %bitcast.8, bf16[4,8,128]{2,1,0:T(8,128)(2,1)} %bitcast.9, s32[1,8]{1,0:T(1,128)} %bitcast.11, ...), custom_call_target="tpu_custom_call" | custom-call | tf_op jit(solution)/shard_map/pallas_call | solution.py:415
  27.6 0.6 %copy.11 = bf16[4,8,320]{2,1,0:T(8,128)(2,1)} copy(bf16[4,8,320]{2,1,0:T(8,128)(2,1)S(1)} %shard_map.91) | data formatting | bytes 40960

commit v5 on v4

--- a/solution.py
+++ b/solution.py
@@ -125,6 +125,9 @@
     partner = {"tensor": home + 1 - core}
     half = groups // 2
     first_mail = late
+    hurry = 4 * z >= planes
+    calm = jnp.where(hurry, 0, 1)
+    quarter = groups // 4
     plane = 2 * (chips - 1)
 
     @pl.when(core != first_mail)
@@ -140,6 +143,7 @@
             k = lax.rem(order + half + away + groups, groups)
             there = k // half
             mail = late + there - 2 * late * there
+            mail = jnp.where(k < quarter, 1 - calm, mail)
             pl.semaphore_signal(
                 barrier,
                 inc=1,
@@ -151,7 +155,10 @@
         lax.fori_loop(0, groups - 1, greet_group, 0)
         for k in range(chips - 1):
             pl.semaphore_signal(
-                barrier, inc=1, device_id={"tensor": chunk_at(k) * 2}, device_id_type=MESH
+                barrier,
+                inc=1,
+                device_id={"tensor": chunk_at(k) * 2 + (1 - late) * (1 - calm)},
+                device_id_type=MESH,
             )
 
     def meet(which, mail, count):
@@ -165,12 +172,14 @@
             pl.semaphore_wait(met_sem.at[which], 1)
 
     def meet_first():
-        meet(0, first_mail, 2 * half + 1 + (1 - late) * (plane - 2))
+        others = jnp.where(hurry, half - 1 + late, quarter - 1)
+        meet(0, first_mail, 2 * others + 1 + calm * plane)
 
     def meet_second():
-        meet(1, 1 - first_mail, 2 * half + late * (plane - 2))
-
-    def send_to(first, which):
+        others = jnp.where(hurry, half - late, groups - quarter)
+        meet(1, 1 - first_mail, 2 * others + (1 - calm) * plane)
+
+    def send_to(first, last, which):
         src, dst = ((down_v, gdown), (up_v, gup))[which]
 
         def send(k, carry):
@@ -184,14 +193,13 @@
             ).start()
             return carry
 
-        lax.fori_loop(first, jnp.clip(order, first, first + half), send, 0)
-        lax.fori_loop(jnp.clip(order + 1, first, first + half), first + half, send, 0)
+        lax.fori_loop(first, jnp.clip(order, first, last), send, 0)
+        lax.fori_loop(jnp.clip(order + 1, first, last), last, send, 0)
 
     def wait_mine():
         for c in mine_copies:
             c.wait()
 
-    hurry = 4 * z >= planes
 
     last = (late == 1) & (4 * z < 3 * planes)
     pl.when(jnp.logical_not(last))(greet)
@@ -202,7 +210,7 @@
     @pl.when(hurry)
     def _():
         meet_first()
-        send_to(0, 0)
+        send_to(0, half, 0)
 
     pl.when(last)(greet)
 
@@ -258,12 +266,12 @@
     attended = jnp.concatenate([mixed[h * toks : (h + 1) * toks] for h in range(QH)], axis=1)
     attended = attended.astype(jnp.bfloat16)
 
-    pl.when(hurry)(lambda: send_to(0, 1))
+    pl.when(hurry)(lambda: send_to(0, half, 1))
 
     @pl.when(late == 1)
     def _():
         meet_second()
-        send_to(half, 0)
+        send_to(half, groups, 0)
 
     for c in w_copies:
         c.wait()
@@ -275,11 +283,16 @@
         keep[k, :, :] = jnp.where(core == 0, first, second)
         send1[k, :, :] = jnp.where(core == 0, second, first).astype(jnp.bfloat16)
 
+    @pl.when(hurry & (late == 0))
+    def _():
+        meet_second()
+        send_to(half, groups, 0)
+
     @pl.when(jnp.logical_not(hurry))
     def _():
         meet_first()
-        send_to(0, 0)
-        send_to(0, 1)
+        send_to(0, quarter, 0)
+        send_to(0, quarter, 1)
 
 
     to_partner = []
@@ -314,10 +327,10 @@
         else:
             total = both
 
-    @pl.when(late == 0)
+    @pl.when(jnp.logical_not(hurry))
     def _():
         meet_second()
-        send_to(half, 0)
+        send_to(quarter, groups, 0)
 
     gdown[order] = down_v[...]
     gup[order] = up_v[...]
@@ -367,7 +380,8 @@
     for copy in low_copies:
         copy.start()
 
-    send_to(half, 1)
+    pl.when(hurry)(lambda: send_to(half, groups, 1))
+    pl.when(jnp.logical_not(hurry))(lambda: send_to(quarter, groups, 1))
     for h in range(2):
         wait_half(1, gup, h)
     for i in range(groups):
@@ -378,6 +392,12 @@
         to_chips[k].wait_recv()
         total = total + recv2[k].astype(jnp.float32)
     others = lows.at[pl.ds(0, tensors - 1)]
+    pltpu.make_async_copy(others, others, low_sent).wait()
+    pltpu.make_async_copy(downs, downs, sent_sem.at[0]).wait()
+    pltpu.make_async_copy(ups, ups, sent_sem.at[1]).wait()
+    for copy in to_partner + to_chips:
+        copy.wait_send()
+
     pltpu.make_async_copy(others, others, low_sem).wait()
     low = lows[0].astype(jnp.float32)
     for d in range(1, tensors):
@@ -386,19 +406,13 @@
     low = jnp.concatenate([jnp.where(left, low, 0.0), jnp.where(left, 0.0, low)], axis=0)
     high = low.astype(jnp.bfloat16)
     rest = (low - high.astype(jnp.float32)).astype(jnp.bfloat16)
-    delta = jnp.dot(high, up, preferred_element_type=jnp.float32) + jnp.dot(
-        rest, up, preferred_element_type=jnp.float32
-    )
+    delta = jnp.dot(
+        jnp.concatenate([high, rest], axis=0), up, preferred_element_type=jnp.float32
+    )
+    delta = delta[:toks] + delta[toks:]
     result = (total + 2.0 * delta).astype(out_ref.dtype)
     for s in range(steps):
         out_ref[s, :, :] = result[s * rows : (s + 1) * rows]
-
-    pltpu.make_async_copy(others, others, low_sent).wait()
-    pltpu.make_async_copy(downs, downs, sent_sem.at[0]).wait()
-    pltpu.make_async_copy(ups, ups, sent_sem.at[1]).wait()
-    for copy in to_partner + to_chips:
-        copy.wait_send()
-
 
 def on_device(mesh_shape, queries, keys, values, step_keys, step_values, lengths, weight, down, up):
     groups, tensors = mesh_shape

time: 28.3 us -> 28.1 us (level)
  Pallas kernels: 27.6 us -> 27.3 us
where the time goes in v5:
time: 28.1 us; the launch traced here: 28 us
  Pallas kernels  27.3 us (97%)
  local copies, waits for them, and re-layouts  0.61 us (2%)
    pallas_call x1, Pallas kernels, on_device(): pl.pallas_call(functools.partial(kernel, groups, tensors), out_shape=pltp...  27.3 us
    unnamed x1, local copies, waits for them, and re-layouts  0.61 us

profile of v5, /device:TPU:1, one launch (start us, length us, event | category | flops | bytes accessed | tf_op | source)
XLA Modules:
  0.0 28.0 jit_solution(12354208941158481746)
XLA Ops:
  0.0 27.3 %shard_map.91 = bf16[4,8,320]{2,1,0:T(8,128)(2,1)S(1)} custom-call(bf16[4,8,256]{2,1,0:T(8,128)(2,1)} %q_hbm.1, bf16[8,512,128]{2,1,0:T(8,128)(2,1)} %bitcast.6, bf16[8,512,128]{2,1,0:T(8,128)(2,1)} %bitcast.7, bf16[4,8,128]{2,1,0:T(8,128)(2,1)} %bitcast.8, bf16[4,8,128]{2,1,0:T(8,128)(2,1)} %bitcast.9, s32[1,8]{1,0:T(1,128)} %bitcast.11, ...), custom_call_target="tpu_custom_call" | custom-call | tf_op jit(solution)/shard_map/pallas_call | solution.py:429
  27.3 0.6 %copy.11 = bf16[4,8,320]{2,1,0:T(8,128)(2,1)} copy(bf16[4,8,320]{2,1,0:T(8,128)(2,1)S(1)} %shard_map.91) | data formatting | bytes 40960

commit v6 on v5

--- a/solution.py
+++ b/solution.py
@@ -204,7 +204,7 @@
     last = (late == 1) & (4 * z < 3 * planes)
     pl.when(jnp.logical_not(last))(greet)
     for c in smalls + k_copies:
-        c.start()
+        c.start(priority=1)
     wait_mine()
 
     @pl.when(hurry)
@@ -215,7 +215,7 @@
     pl.when(last)(greet)
 
     for c in v_copies + w_copies:
-        c.start()
+        c.start(priority=1)
 
     for c in smalls:
         c.wait()

time: 28.1 us -> 28.1 us (level)
  no operation moved by 1% of the time
where the time goes in v6:
time: 28.1 us; the launch traced here: 28 us
  Pallas kernels  27.3 us (97%)
  local copies, waits for them, and re-layouts  0.61 us (2%)
    pallas_call x1, Pallas kernels, on_device(): pl.pallas_call(functools.partial(kernel, groups, tensors), out_shape=pltp...  27.3 us
    unnamed x1, local copies, waits for them, and re-layouts  0.61 us

profile of v6, /device:TPU:1, one launch (start us, length us, event | category | flops | bytes accessed | tf_op | source)
XLA Modules:
  0.0 28.0 jit_solution(14324106407217257629)
XLA Ops:
  0.0 27.3 %shard_map.91 = bf16[4,8,320]{2,1,0:T(8,128)(2,1)S(1)} custom-call(bf16[4,8,256]{2,1,0:T(8,128)(2,1)} %q_hbm.1, bf16[8,512,128]{2,1,0:T(8,128)(2,1)} %bitcast.6, bf16[8,512,128]{2,1,0:T(8,128)(2,1)} %bitcast.7, bf16[4,8,128]{2,1,0:T(8,128)(2,1)} %bitcast.8, bf16[4,8,128]{2,1,0:T(8,128)(2,1)} %bitcast.9, s32[1,8]{1,0:T(1,128)} %bitcast.11, ...), custom_call_target="tpu_custom_call" | custom-call | tf_op jit(solution)/shard_map/pallas_call | solution.py:429
  27.3 0.6 %copy.11 = bf16[4,8,320]{2,1,0:T(8,128)(2,1)} copy(bf16[4,8,320]{2,1,0:T(8,128)(2,1)S(1)} %shard_map.91) | data formatting | bytes 40960

commit v7 on v6

--- a/solution.py
+++ b/solution.py
@@ -203,7 +203,7 @@
 
     last = (late == 1) & (4 * z < 3 * planes)
     pl.when(jnp.logical_not(last))(greet)
-    for c in smalls + k_copies:
+    for c in smalls + k_copies + v_copies + w_copies:
         c.start(priority=1)
     wait_mine()
 
@@ -213,9 +213,6 @@
         send_to(0, half, 0)
 
     pl.when(last)(greet)
-
-    for c in v_copies + w_copies:
-        c.start(priority=1)
 
     for c in smalls:
         c.wait()

time: 28.1 us -> 29 us (1.032)
  Pallas kernels: 27.3 us -> 28.2 us
    pallas_call x1, Pallas kernels: 27.3 us -> 28.2 us  [on_device(): pl.pallas_call(functools.partial(kernel, groups, tensors), out_shape=pltp...]
where the time goes in v7:
time: 29 us; the launch traced here: 28.8 us
  Pallas kernels  28.2 us (97%)
  local copies, waits for them, and re-layouts  0.61 us (2%)
    pallas_call x1, Pallas kernels, on_device(): pl.pallas_call(functools.partial(kernel, groups, tensors), out_shape=pltp...  28.2 us
    unnamed x1, local copies, waits for them, and re-layouts  0.61 us

profile of v7, /device:TPU:1, one launch (start us, length us, event | category | flops | bytes accessed | tf_op | source)
XLA Modules:
  0.0 28.8 jit_solution(15250619419423329914)
XLA Ops:
  0.0 28.2 %shard_map.91 = bf16[4,8,320]{2,1,0:T(8,128)(2,1)S(1)} custom-call(bf16[4,8,256]{2,1,0:T(8,128)(2,1)} %q_hbm.1, bf16[8,512,128]{2,1,0:T(8,128)(2,1)} %bitcast.6, bf16[8,512,128]{2,1,0:T(8,128)(2,1)} %bitcast.7, bf16[4,8,128]{2,1,0:T(8,128)(2,1)} %bitcast.8, bf16[4,8,128]{2,1,0:T(8,128)(2,1)} %bitcast.9, s32[1,8]{1,0:T(1,128)} %bitcast.11, ...), custom_call_target="tpu_custom_call" | custom-call | tf_op jit(solution)/shard_map/pallas_call | solution.py:426
  28.2 0.6 %copy.11 = bf16[4,8,320]{2,1,0:T(8,128)(2,1)} copy(bf16[4,8,320]{2,1,0:T(8,128)(2,1)S(1)} %shard_map.91) | data formatting | bytes 40960
